TPU v7x, 256 devices: a whole 4x4x8 slice. The times are simulated.
256 devices in a mesh: pat: 32 (over x, y, core), code: 8 (over z).
Axes of the slice: x: 4, y: 4, z: 8, core: 2. Of those that a mesh axis runs over, the one named last changes fastest.
Arguments:
- visit_codes: bfloat16 [2048, 128, 4096], P('pat', None, 'code'), may hold values from -6 to 6
- slice_length: int32 [512], P('pat'), may hold values from 16 to 512, as said below
- code_factor: bfloat16 [4096, 128], P('code'), may hold values from -0.09375 to 0.09375
- mix_factor: bfloat16 [128, 128], replicated, may hold values from -0.5 to 0.5
- slice_weight: float32 [512, 128], P('pat'), may hold values from 0.3 to 3
Outputs:
- mttkrp_mix: float32 [128, 128], replicated
- mttkrp_code: float32 [4096, 128], P('code')
- mttkrp_slice: float32 [512, 128], P('pat')
Inputs may be any that keep to these rules, and one draw needn't show every extreme that they name: `slice_length`: every index of pat holds 16 slices whose buckets fit its 64 slots; some slice has exactly 512 visits and some exactly 16.
All inputs are finite; a program needn't handle non-finite values.
Results may differ from a plain program's by a relative error of at most 0.0011.
Values may be sent and summed in bfloat16 or wider, within the bound.
A program may use at most 128 MiB of HBM per device.

v0:
```python
import jax
import jax.numpy as jnp
from jax import lax
from jax.sharding import PartitionSpec as P

NS_STEPS = 8


HIGH = lax.Precision.HIGHEST


def layout(lengths, slots_all, rows_per):
    counts = (lengths + rows_per - 1) // rows_per
    ends = jnp.cumsum(counts)
    starts = ends - counts
    slots = jnp.arange(slots_all, dtype=jnp.int32)[:, None]
    member = (slots >= starts[None, :]) & (slots < ends[None, :])
    owner = member.astype(jnp.float32)
    first = jnp.sum(jnp.where(member, starts[None, :], 0), axis=1)
    length = jnp.sum(jnp.where(member, lengths[None, :], 0), axis=1)
    rowpos = (
        jnp.arange(slots_all, dtype=jnp.int32)[:, None] - first[:, None]
    ) * rows_per + jnp.arange(rows_per, dtype=jnp.int32)[None, :]
    return (owner, rowpos < length[:, None])


def newton_schulz(grams):
    trace = jnp.trace(grams, axis1=1, axis2=2) + 1e-06
    ident = jnp.eye(grams.shape[1], dtype=jnp.float32)
    multi = ident[None] / jnp.sqrt(trace)[:, None, None]
    for step in range(NS_STEPS):
        inner = jnp.einsum("kar,kab,kbs->krs", multi, grams, multi, precision=HIGH)
        multi = jnp.einsum("kar,krs->kas", multi, 1.5 * ident[None] - 0.5 * inner, precision=HIGH)
    return multi


def shards(visit_codes, slice_length, code_factor, mix_factor, slice_weight):
    slots_all, rows_per, width = visit_codes.shape
    rank = mix_factor.shape[0]
    owner, live = layout(slice_length, slots_all, rows_per)
    masked = jnp.where(live[:, :, None], visit_codes, jnp.zeros_like(visit_codes))
    flat = masked.reshape(-1, width)
    partial_a = jnp.dot(flat, code_factor, preferred_element_type=jnp.float32)
    mix32 = mix_factor.astype(jnp.float32)
    rowscale = jnp.dot(owner, slice_weight, precision=HIGH)
    local_a = lax.psum(partial_a, "code")
    summed3 = local_a.reshape(-1, rows_per, rank)
    mapped = jnp.einsum("bir,ar->bia", summed3 * rowscale[:, None, :], mix32, precision=HIGH)
    gram_b = jnp.einsum("bir,bis->brs", mapped, mapped, precision=HIGH)
    grams = jnp.einsum("bk,brs->krs", owner, gram_b, precision=HIGH)
    multi = newton_schulz(grams)
    multi_b = jnp.einsum("bk,krs->brs", owner, multi, precision=HIGH)
    polar = jnp.einsum("bir,brs->bis", mapped, multi_b, precision=HIGH).astype(jnp.bfloat16)
    cross_b = jnp.einsum("bir,bis->brs", polar.astype(jnp.float32), summed3, precision=HIGH)
    cross = jnp.einsum("bk,brs->krs", owner, cross_b, precision=HIGH)
    mix_part = jnp.sum(cross * slice_weight[:, None, :], axis=0)
    slice_out = jnp.sum(mix32[None] * cross, axis=1)
    upper = jnp.dot(polar.reshape(-1, rank), mix_factor, preferred_element_type=jnp.float32)
    upper = (
        (upper.reshape(-1, rows_per, rank) * rowscale[:, None, :])
        .astype(jnp.bfloat16)
        .reshape(-1, rank)
    )
    code_part = lax.dot_general(
        flat, upper, (((0,), (0,)), ((), ())), preferred_element_type=jnp.float32
    )
    code_out, mix_out = lax.psum((code_part, mix_part), "pat")
    return (mix_out, code_out, slice_out)


def solution(mesh):
    in_specs = (P("pat", None, "code"), P("pat"), P("code", None), P(), P("pat", None))
    out_specs = (P(), P("code", None), P("pat", None))
    return jax.shard_map(shards, mesh=mesh, in_specs=in_specs, out_specs=out_specs, check_vma=False)
```

profile of v0, /device:TPU:1, one launch (start us, length us, event | category | flops | bytes accessed | tf_op | source)
XLA Modules:
  0.0 331.7 jit_solution(12971554922913653354)
XLA Ops:
  7.2 0.7 fusion.120
  7.9 0.1 copy.10
  8.0 0.1 reduce
  8.2 0.7 fusion.119
  8.8 0.7 select_reduce_fusion.2
  9.6 0.1 add_compare_fusion
  9.7 4.7 %broadcast_select_fusion = bf16[64,128,512]{2,1,0:T(8,128)(2,1)S(1)} fusion(bf16[64,128,512]{2,1,0:T(8,128)(2,1)} %param.5, pred[64,128]{1,0:T(8,128)(4,1)S(1)} %add_compare_fusion), kind=kLoop, calls=%fused_computation | loop fusion | flops 4194304 | bytes 16785408 | tf_op jit(solution)/shard_map/jit(_where)/select_n | solution.py:41
  14.4 4.5 %fusion.47 = f32[8192,128]{1,0:T(8,128)} fusion(bf16[8192,512]{1,0:T(8,128)(2,1)S(1)} %bitcast.78, bf16[512,128]{1,0:T(8,128)(2,1)S(1)} %copy-done), kind=kOutput, calls=%fused_computation.66 | convolution fusion | flops 1073741824 | bytes 12713984 | tf_op jit(solution)/shard_map/dot_general | solution.py:43
  18.9 0.0 all-reduce.6.cloned.1.call-start
  18.9 0.7 copy-done.5
  19.7 0.3 fusion.45
  19.9 111.9 %all-reduce.4.cloned.1.call-done = f32[64,128,128]{2,1,0:T(8,128)} async-done(((f32[64,128,128]{2,1,0:T(8,128)}), f32[64,128,128]{2,1,0:T(8,128)}) %all-reduce.4.cloned.1.call-update) | async-done | bytes 4194320 | tf_op jit(solution)/shard_map/psum | solution.py:46
  131.8 4.2 %fusion.6 = f32[64,128,128]{2,1,0:T(8,128)S(1)} fusion(f32[64,128,128]{2,1,0:T(8,128)} %all-reduce.4.cloned.1.call-done, f32[64,128]{1,0:T(8,128)S(1)} %fusion.45, bf16[128,128]{1,0:T(8,128)(2,1)S(1)} %copy-done.5), kind=kOutput, calls=%fused_computation.8 | convolution fusion | flops 1611661312 | bytes 8454144 | tf_op jit(solution)/shard_map/bir,ar->bia/dot_general | solution.py:48
  136.0 7.2 %fusion.48 = f32[64,128,128]{2,1,0:T(8,128)S(1)} fusion(f32[64,128,128]{2,1,0:T(8,128)S(1)} %fusion.6), kind=kOutput, calls=%fused_computation.67 | convolution fusion | flops 1610612736 | bytes 8388608 | tf_op jit(solution)/shard_map/bir,bis->brs/dot_general | solution.py:49
  143.2 4.1 %select_reduce_fusion = (f32[16]{0:T(128)S(1)}, f32[16,128,128]{2,0,1:T(8,128)S(1)}) fusion(pred[128,128]{1,0:T(8,128)(4,1)S(1)} %iota_compare_fusion, f32[64,128,128]{2,1,0:T(8,128)S(1)} %fusion.48, s32[16]{0:T(128)S(1)} %reduce, s32[16]{0:T(128)S(1)} %fusion.119), kind=kOutput, calls=%fused_computation.33 | convolution fusion | flops 201853936 | bytes 5259456 | tf_op jit(solution)/shard_map/bk,brs->krs/dot_general | solution.py:50
  147.3 0.4 copy.13
  147.8 1.7 fusion.25
  149.5 1.9 fusion.19
  151.4 1.2 fusion.22
  152.6 1.2 fusion.49
  153.8 1.9 fusion.18
  155.7 1.2 fusion.50
  156.9 1.2 fusion.51
  158.1 1.9 fusion.17
  160.1 1.4 fusion.52
  161.4 1.2 fusion.53
  162.6 1.9 fusion.16
  164.5 1.2 fusion.54
  165.7 1.2 fusion.55
  166.9 1.9 fusion.15
  168.9 1.2 fusion.56
  170.0 1.2 fusion.57
  171.2 2.1 fusion.14
  173.4 1.2 fusion.58
  174.6 1.2 fusion.59
  175.8 1.9 fusion.13
  177.7 1.2 fusion.60
  178.9 1.2 fusion.61
  180.1 1.9 fusion.12
  182.0 1.2 fusion.62
  183.2 2.6 fusion.20
  185.8 7.9 %fusion.9 = bf16[64,128,128]{2,1,0:T(8,128)(2,1)S(1)} fusion(f32[64,128,128]{2,1,0:T(8,128)S(1)} %copy-done.3, f32[64,128,128]{2,0,1:T(8,128)S(1)} %fusion.20), kind=kOutput, calls=%fused_computation.11 | convolution fusion | flops 1611661312 | bytes 10485760 | tf_op jit(solution)/shard_map/bir,brs->bis/dot_general | solution.py:53
  193.7 7.5 %convolution_bitcast_fusion = f32[512,128]{1,0:T(8,128)} fusion(bf16[64,128,512]{2,1,0:T(8,128)(2,1)} %copy-done.4, bf16[64,128,128]{2,1,0:T(8,128)(2,1)S(1)} %fusion.9, f32[64,128]{1,0:T(8,128)S(1)} %fusion.45, bf16[128,128]{1,0:T(8,128)(2,1)S(1)} %copy-done.5), kind=kOutput, calls=%fused_computation.28 | convolution fusion | flops 1344274432 | bytes 10813440 | tf_op jit(solution)/shard_map/dot_general | solution.py:64
  201.2 4.8 %fusion.63 = f32[64,128,128]{2,1,0:T(8,128)S(1)} fusion(bf16[64,128,128]{2,1,0:T(8,128)(2,1)S(1)} %fusion.9, f32[64,128,128]{2,1,0:T(8,128)} %all-reduce.4.cloned.1.call-done), kind=kOutput, calls=%fused_computation.82 | convolution fusion | flops 1610612736 | bytes 10485760 | tf_op jit(solution)/shard_map/bir,bis->brs/dot_general | solution.py:54
  205.9 4.7 %multiply_reduce_fusion = (f32[16,128]{1,0:T(8,128)}, f32[128,128]{1,0:T(8,128)}) fusion(f32[128,128]{1,0:T(8,128)S(1)} %convert_element_type.22, f32[16,128]{1,0:T(8,128)S(1)} %copy-done.6, f32[64,128,128]{2,1,0:T(8,128)S(1)} %fusion.63, s32[16]{0:T(128)S(1)} %reduce, s32[16]{0:T(128)S(1)} %fusion.119), kind=kOutput, calls=%fused_computation.31 | convolution fusion | flops 202359808 | bytes 4341888 | tf_op jit(solution)/shard_map/bk,brs->krs/dot_general | solution.py:55
  210.7 110.9 %all-reduce.6.cloned.1.call-done = (f32[128,128]{1,0:T(8,128)}, f32[512,128]{1,0:T(8,128)}) async-done(((f32[128,128]{1,0:T(8,128)}, f32[512,128]{1,0:T(8,128)}), (f32[128,128]{1,0:T(8,128)}, f32[512,128]{1,0:T(8,128)})) %all-reduce.6.cloned.1.call-update) | async-done | bytes 327696 | tf_op jit(solution)/shard_map/psum | solution.py:67
  321.6 1.5 copy.35
  323.0 1.7 copy.36
  (23 shorter events, 0.2 us)
Async XLA Ops:
  7.2 7.2 %copy-start = (bf16[512,128]{1,0:T(8,128)(2,1)S(1)}, bf16[512,128]{1,0:T(8,128)(2,1)}, u32[]{:S(2)}) copy-start(bf16[512,128]{1,0:T(8,128)(2,1)} %param.7) | copy-start | bytes 393220
  7.2 124.6 %all-reduce.4.cloned.1.call-start = ((), (), s32[]{:S(2)}) async-start(), calls=%async_computation | async-start | bytes 8388608 | tf_op jit(solution)/shard_map/psum | solution.py:46
  14.4 4.5 %copy-start.4 = (bf16[64,128,512]{2,1,0:T(8,128)(2,1)}, bf16[64,128,512]{2,1,0:T(8,128)(2,1)S(1)}, u32[]{:S(2)}) copy-start(bf16[64,128,512]{2,1,0:T(8,128)(2,1)S(1)} %broadcast_select_fusion) | copy-start | bytes 25165828
  18.8 0.8 copy-start.5
  18.8 0.8 copy-start.6
  18.9 302.7 %all-reduce.6.cloned.1.call-start = ((), (), s32[]{:S(2)}) async-start(), calls=%async_computation.1 | async-start | bytes 655360 | tf_op jit(solution)/shard_map/psum | solution.py:67
  136.0 7.3 %copy-start.2 = (f32[64,128,128]{2,1,0:T(8,128)}, f32[64,128,128]{2,1,0:T(8,128)S(1)}, u32[]{:S(2)}) copy-start(f32[64,128,128]{2,1,0:T(8,128)S(1)} %fusion.6) | copy-start | bytes 12582916
  182.0 3.8 %copy-start.3 = (f32[64,128,128]{2,1,0:T(8,128)S(1)}, f32[64,128,128]{2,1,0:T(8,128)}, u32[]{:S(2)}) copy-start(f32[64,128,128]{2,1,0:T(8,128)} %copy-done.2) | copy-start | bytes 12582916
  201.2 123.5 %copy-start.1 = (bf16[512,128]{1,0:T(8,128)(2,1)S(1)}, bf16[512,128]{1,0:T(8,128)(2,1)}, u32[]{:S(2)}) copy-start(bf16[512,128]{1,0:T(8,128)(2,1)} %param.7) | copy-start | bytes 393220
Sparse Core Ops, SparseCore 0:
  19.0 112.7 all-reduce.3
  210.8 110.6 all-reduce.5
where the time goes:
time: 336 us; the launch traced here: 332 us
  waiting for transfers between devices  223 us (66%)
  matrix products  82.9 us (25%)
  between operations  14.6 us (4%)
  other arithmetic  7.06 us (2%)
  local copies, waits for them, and re-layouts  4.36 us (1%)
    psum x1, waiting for transfers between devices, shards(): local_a = lax.psum(partial_a, 'code')  112 us
    psum x1, waiting for transfers between devices, shards(): code_out, mix_out = lax.psum((code_part, mix_part), 'pat')  111 us
    dot_general x16, matrix products, newton_schulz(): inner = jnp.einsum('kar,kab,kbs->krs', multi, grams, multi, precision=HIGH)  25.6 us
    dot_general x8, matrix products, newton_schulz(): jnp.einsum('kar,krs->kas', multi, 1.5 * ident[None] - 0.5 * inner, precis...  9.68 us
    dot_general x1, matrix products, shards(): jnp.einsum('bir,brs->bis', mapped, multi_b, precision=HIGH)  7.87 us
    dot_general x1, matrix products, shards(): lax.dot_general(flat, upper, (((0,), (0,)), ((), ())), preferred_element_...  7.47 us
    dot_general x1, matrix products, shards(): gram_b = jnp.einsum('bir,bis->brs', mapped, mapped, precision=HIGH)  7.24 us
  transfers between devices with their start and end apart: 2, of which 2 were waited for; matrix products, arithmetic and copies ran while one was open for 0% of the time, Pallas kernels for 0%

commit v1 on v0

v1 whole, which is shorter than its diff:
```python
import functools
import jax
import jax.numpy as jnp
from jax import lax
from jax.experimental import pallas as pl
from jax.experimental.pallas import tpu as pltpu
from jax.sharding import PartitionSpec as P

NS_STEPS = 8
MESH = pl.DeviceIdType.MESH
F32 = jnp.float32
BF16 = jnp.bfloat16


def dot(a, b):
    return jnp.dot(a, b, preferred_element_type=F32)


def split(a):
    high = a.astype(BF16)
    return high, (a - high.astype(F32)).astype(BF16)


def mm3(a, b):
    ah, al = split(a)
    bh, bl = split(b)
    return dot(ah, bh) + (dot(ah, bl) + dot(al, bh))


def encode(rows):
    grouped = rows.reshape(4, 32, 128)
    top = jnp.maximum(jnp.max(jnp.abs(grouped), axis=1), 1e-30)
    power = jnp.floor(jnp.log2(top) + 0.001) + 1.0
    factor = jnp.exp2(14.0 - power)
    codes = jnp.round(grouped * factor[:, None, :]).astype(jnp.int32)
    return codes.reshape(128, 128).astype(jnp.int16), power


def kernel(n_pat, n_code, x_hbm, len_ref, v_ref, h_ref, d_ref,
           mix_ref, code_ref, slice_ref,
           xv, ap, starts, rs_send, rs_recv, a_sum, u_own, u_recv, acc,
           mixp, m1, mz, m2, m3, slp, slr, acct, cbuf, hsum, rbuf,
           x_sem, rs_ss, rs_rs, ag_ss, ag_rs, m1_ss, m1_rs, m2_ss, m2_rs,
           m3_ss, m3_rs, m4_ss, m4_rs, sl_ss, sl_rs, c_ss, c_rs, r_ss, r_rs,
           g_ss, g_rs, f_ss, f_rs):
    pat = lax.axis_index("pat")
    me = lax.axis_index("code")
    chips = n_pat // 2
    chip, core = pat // 2, pat % 2
    other = pat + 1 - 2 * core

    def z_at(off):
        return lax.rem(me + off + n_code, n_code)

    def chip_at(off):
        return lax.rem(chip + off + chips, chips)

    barrier = pltpu.get_barrier_semaphore()
    for off in range(1, n_code):
        pl.semaphore_signal(barrier, inc=1, device_id=(pat, z_at(off)), device_id_type=MESH)
    pl.semaphore_signal(barrier, inc=1, device_id=(other, me), device_id_type=MESH)
    for off in range(1, chips):
        pl.semaphore_signal(barrier, inc=1, device_id=(chip_at(off) * 2 + core, me), device_id_type=MESH)

    def x_copy(i):
        part = pl.ds(i * 4, 4)
        return pltpu.make_async_copy(x_hbm.at[part], xv.at[part], x_sem.at[i])

    for i in range(16):
        x_copy(i).start()
    at = jnp.int32(0)
    for k in range(16):
        starts[k] = at
        at = at + (len_ref[k] + 127) // 128

    @pl.loop(0, 16)
    def _(i):
        x_copy(i).wait()
        part = pl.ds(i * 4, 4)
        ap[part] = dot(xv[part].reshape(512, 512), v_ref[...]).reshape(4, 128, 128)

    pl.semaphore_wait(barrier, n_code - 1 + chips)

    rowpos = lax.broadcasted_iota(jnp.int32, (128, 128), 0)

    def own(s, j):
        block = ap[jnp.minimum(starts[s] + j, 63)]
        return jnp.where(rowpos < len_ref[s] - j * 128, block, 0.0)

    def received(buf, j):
        power = buf[512:528].astype(jnp.int32).astype(F32)[4 * j:4 * j + 4]
        codes = buf[128 * j:128 * j + 128].astype(jnp.int32).astype(F32)
        return (codes.reshape(4, 32, 128) * jnp.exp2(power - 14.0)[:, None, :]).reshape(128, 128)

    def rs_copy(way, step, half):
        to = z_at(1) if way == 0 else z_at(-1)
        at = (way * 4 + step) * 2 + half
        return pltpu.make_async_remote_copy(
            src_ref=rs_send.at[at], dst_ref=rs_recv.at[at],
            send_sem=rs_ss.at[at], recv_sem=rs_rs.at[at],
            device_id=(pat, to), device_id_type=MESH)

    def rs_message(way, step, half):
        dest = z_at(4 - step) if way == 0 else z_at(step - 4)
        first = 0 if half == way else 1
        if step > first:
            rs_copy(way, step - 1, half).wait_recv()
        at = (way * 4 + step) * 2 + half
        powers = []
        for j in range(4):
            rows = own(dest * 2 + half, j)
            if step > first:
                rows = rows + received(rs_recv.at[at - 2], j)
            codes, power = encode(rows)
            rs_send[at, 128 * j:128 * j + 128] = codes
            powers.append(power)
        rs_send[at, 512:528] = jnp.concatenate(powers, axis=0).astype(jnp.int32).astype(jnp.int16)
        rs_copy(way, step, half).start()

    rs_message(0, 0, 0)
    rs_message(1, 0, 1)
    for step in range(1, 4):
        rs_message(0, step, 1)
        rs_message(1, step, 0)
        rs_message(0, step, 0)
        rs_message(1, step, 1)

    eye = (rowpos == lax.broadcasted_iota(jnp.int32, (128, 128), 1)).astype(F32)
    h32 = h_ref[...].astype(F32)
    ht = h32.T.astype(BF16)
    hd, hdt, dcol, drow = [], [], [], []
    for half in range(2):
        drow.append(d_ref[pl.ds(me * 2 + half, 1), :])
        hd.append(h32 * drow[half])
        hdt.append(hd[half].T)
        dcol.append(jnp.sum(eye * drow[half], axis=1, keepdims=True))

    grams = []
    for half in (1, 0):
        rs_copy(0, 3, half).wait_recv()
        rs_copy(1, 3, half).wait_recv()
        for j in range(4):
            rows = own(me * 2 + half, j)
            rows = rows + received(rs_recv.at[6 + half], j)
            rows = rows + received(rs_recv.at[14 + half], j)
            a_sum[half, 128 * j:128 * j + 128] = rows
    ahs, als, aths, atls = [], [], [], []
    for half in range(2):
        ah, al = split(a_sum[half])
        ath, atl = split(a_sum[half].T)
        ahs.append(ah)
        als.append(al)
        aths.append(ath)
        atls.append(atl)
        cross = dot(ath, al)
        b = dot(ath, ah) + (cross + dot(atl, ah))
        grams.append(mm3(mm3(hd[half], b), hdt[half]))

    zs, ps = [], []
    roots = []
    for half in range(2):
        trace = jnp.sum(grams[half] * eye, keepdims=True) + 1e-06
        zs.append(grams[half] / trace)
        roots.append(1.0 / jnp.sqrt(trace))
    for step in range(NS_STEPS):
        ss = [1.5 * eye - 0.5 * z for z in zs]
        if step < NS_STEPS - 1:
            zs = [mm3(z, s) for z, s in zip(zs, ss)]
        if step == 0:
            ps = [s * r for s, r in zip(ss, roots)]
        else:
            ps = [mm3(p, s) for p, s in zip(ps, ss)]
        if step < NS_STEPS - 1:
            zs = [mm3(z, s) for z, s in zip(zs, ss)]

    qts = []
    for half in range(2):
        rh, rl = split(mm3(ps[half], hd[half]))
        q = dot(rh, aths[half]) + (dot(rh, atls[half]) + dot(rl, aths[half]))
        q = q.astype(BF16)
        qts.append(q)
        u_own[half] = (dot(ht, q) * dcol[half]).astype(BF16)

    def ag_copy(way, step, half):
        to = z_at(1) if way == 0 else z_at(-1)
        at = (way * 4 + step) * 2 + half
        src = u_own.at[half] if step == 0 else u_recv.at[at - 2]
        return pltpu.make_async_remote_copy(
            src_ref=src, dst_ref=u_recv.at[at],
            send_sem=ag_ss.at[at], recv_sem=ag_rs.at[at],
            device_id=(pat, to), device_id_type=MESH)

    ag_copy(0, 0, 0).start()
    ag_copy(1, 0, 1).start()
    ag_copy(0, 0, 1).start()
    ag_copy(1, 0, 0).start()

    def code_term(u, s):
        first = starts[s]
        x = jnp.concatenate([xv[jnp.minimum(first + j, 63)] for j in range(4)], axis=0)
        return dot(u, x)

    ws = [dot(qts[half], ahs[half]) + dot(qts[half], als[half]) for half in range(2)]
    mixp[...] = ws[0] * drow[0] + ws[1] * drow[1]
    slp[...] = jnp.concatenate(
        [jnp.sum(h32 * ws[half], axis=0, keepdims=True) for half in range(2)]
        + [jnp.zeros((6, 128), F32)], axis=0)

    def sl_copy(off):
        return pltpu.make_async_remote_copy(
            src_ref=slp, dst_ref=slr.at[off - 1], send_sem=sl_ss.at[off - 1], recv_sem=sl_rs.at[off - 1],
            device_id=(pat, z_at(off)), device_id_type=MESH)

    def m1_copy(off):
        to = z_at(off)
        return pltpu.make_async_remote_copy(
            src_ref=mixp.at[pl.ds(pl.multiple_of(to * 16, 16), 16)], dst_ref=m1.at[off - 1],
            send_sem=m1_ss.at[off - 1], recv_sem=m1_rs.at[off - 1],
            device_id=(pat, to), device_id_type=MESH)

    def m2_copy():
        return pltpu.make_async_remote_copy(
            src_ref=mz, dst_ref=m2, send_sem=m2_ss, recv_sem=m2_rs,
            device_id=(other, me), device_id_type=MESH)

    def m3_copy(off, sender):
        return pltpu.make_async_remote_copy(
            src_ref=m3.at[sender], dst_ref=m3.at[sender],
            send_sem=m3_ss.at[off - 1], recv_sem=m3_rs.at[off - 1],
            device_id=(chip_at(off) * 2 + core, me), device_id_type=MESH)

    def m4_copy(off, rows):
        part = pl.ds(pl.multiple_of(rows * 16, 16), 16)
        return pltpu.make_async_remote_copy(
            src_ref=mix_ref.at[part], dst_ref=mix_ref.at[part],
            send_sem=m4_ss.at[off - 1], recv_sem=m4_rs.at[off - 1],
            device_id=(pat, z_at(off)), device_id_type=MESH)

    for off in range(1, n_code):
        m1_copy(off).start()
        sl_copy(off).start()

    acc[...] = code_term(u_own[0], me * 2) + code_term(u_own[1], me * 2 + 1)

    for step in range(4):
        for way, half in ((0, 0), (1, 1), (0, 1), (1, 0)):
            if step == 3 and half != way:
                continue
            ag_copy(way, step, half).wait_recv()
            if step < 2 or (step == 2 and half == way):
                ag_copy(way, step + 1, half).start()
            owner = z_at(-step - 1) if way == 0 else z_at(step + 1)
            acc[...] += code_term(u_recv[(way * 4 + step) * 2 + half], owner * 2 + half)
        if step == 0:
            total = mixp[pl.ds(pl.multiple_of(me * 16, 16), 16), :]
            for off in range(1, n_code):
                m1_copy(off).wait_recv()
                total = total + m1[off - 1]
            mz[...] = total
            m2_copy().start()
            slice_ref[me] = slp[0:2]
            for off in range(1, n_code):
                sl_copy(off).wait_recv()
                slice_ref[z_at(-off)] = slr[off - 1, 0:2]
        if step == 1:
            m2_copy().wait_recv()
            m3[chip] = mz[...] + m2[...]
            for off in range(1, chips):
                m3_copy(off, chip).start()
        if step == 2:
            for off in range(1, chips):
                m3_copy(off, chip_at(-off)).wait_recv()
            total = m3[0]
            for c in range(1, chips):
                total = total + m3[c]
            mix_ref[pl.ds(pl.multiple_of(me * 16, 16), 16), :] = total
            for off in range(1, n_code):
                m4_copy(off, me).start()

    acct[...] = acc[...].T.reshape(2, 256, 128)
    core_copy = pltpu.make_async_remote_copy(
        src_ref=acct.at[1 - core], dst_ref=cbuf, send_sem=c_ss, recv_sem=c_rs,
        device_id=(other, me), device_id_type=MESH)
    core_copy.start()
    core_copy.wait_recv()
    hsum[...] = (acct[core] + cbuf[...]).reshape(chips, 256 // chips, 128)

    def r_copy(off):
        to = chip_at(off)
        return pltpu.make_async_remote_copy(
            src_ref=hsum.at[to], dst_ref=rbuf.at[off - 1],
            send_sem=r_ss.at[off - 1], recv_sem=r_rs.at[off - 1],
            device_id=(to * 2 + core, me), device_id_type=MESH)

    for off in range(1, chips):
        r_copy(off).start()
    total = hsum[chip]
    for off in range(1, chips):
        r_copy(off).wait_recv()
        total = total + rbuf[off - 1]
    code_ref[core, chip] = total

    def g_copy(off, sender):
        return pltpu.make_async_remote_copy(
            src_ref=code_ref.at[core, sender], dst_ref=code_ref.at[core, sender],
            send_sem=g_ss.at[off - 1], recv_sem=g_rs.at[off - 1],
            device_id=(chip_at(off) * 2 + core, me), device_id_type=MESH)

    for off in range(1, chips):
        g_copy(off, chip).start()
    for off in range(1, chips):
        g_copy(off, chip_at(-off)).wait_recv()

    def f_copy(half):
        return pltpu.make_async_remote_copy(
            src_ref=code_ref.at[half], dst_ref=code_ref.at[half], send_sem=f_ss, recv_sem=f_rs,
            device_id=(other, me), device_id_type=MESH)

    f_copy(core).start()
    for off in range(1, n_code):
        m4_copy(off, z_at(-off)).wait_recv()

    for way in range(2):
        for step in range(4):
            for half in range(2):
                if half == way or step > 0:
                    rs_copy(way, step, half).wait_send()
                if half == way or step < 3:
                    ag_copy(way, step, half).wait_send()
    for off in range(1, n_code):
        m1_copy(off).wait_send()
        sl_copy(off).wait_send()
        m4_copy(off, me).wait_send()
    m2_copy().wait_send()
    core_copy.wait_send()
    for off in range(1, chips):
        m3_copy(off, chip).wait_send()
        r_copy(off).wait_send()
        g_copy(off, chip).wait_send()
    f_copy(core).wait_send()
    f_copy(1 - core).wait_recv()


def shards(n_pat, n_code, visit_codes, slice_length, code_factor, mix_factor, slice_weight):
    chips = n_pat // 2
    vmem = pl.BlockSpec(memory_space=pltpu.VMEM)
    dma = pltpu.SemaphoreType.DMA
    mix, code, slices = pl.pallas_call(
        functools.partial(kernel, n_pat, n_code),
        out_shape=(
            jax.ShapeDtypeStruct((128, 128), F32),
            jax.ShapeDtypeStruct((2, chips, 256 // chips, 128), F32),
            jax.ShapeDtypeStruct((n_code, 2, 128), F32),
        ),
        in_specs=[pl.BlockSpec(memory_space=pl.ANY), pl.BlockSpec(memory_space=pltpu.SMEM), vmem, vmem, vmem],
        out_specs=(vmem, vmem, vmem),
        scratch_shapes=[
            pltpu.VMEM((64, 128, 512), BF16),
            pltpu.VMEM((64, 128, 128), F32),
            pltpu.SMEM((16,), jnp.int32),
            pltpu.VMEM((16, 528, 128), jnp.int16),
            pltpu.VMEM((16, 528, 128), jnp.int16),
            pltpu.VMEM((2, 512, 128), F32),
            pltpu.VMEM((2, 128, 512), BF16),
            pltpu.VMEM((16, 128, 512), BF16),
            pltpu.VMEM((128, 512), F32),
            pltpu.VMEM((128, 128), F32),
            pltpu.VMEM((n_code - 1, 16, 128), F32),
            pltpu.VMEM((16, 128), F32),
            pltpu.VMEM((16, 128), F32),
            pltpu.VMEM((chips, 16, 128), F32),
            pltpu.VMEM((8, 128), F32),
            pltpu.VMEM((n_code - 1, 8, 128), F32),
            pltpu.VMEM((2, 256, 128), F32),
            pltpu.VMEM((256, 128), F32),
            pltpu.VMEM((chips, 256 // chips, 128), F32),
            pltpu.VMEM((chips - 1, 256 // chips, 128), F32),
            dma((16,)),
            dma((16,)), dma((16,)),
            dma((16,)), dma((16,)),
            dma((n_code - 1,)), dma((n_code - 1,)),
            dma, dma,
            dma((chips - 1,)), dma((chips - 1,)),
            dma((n_code - 1,)), dma((n_code - 1,)),
            dma((n_code - 1,)), dma((n_code - 1,)),
            dma, dma,
            dma((chips - 1,)), dma((chips - 1,)),
            dma((chips - 1,)), dma((chips - 1,)),
            dma, dma,
        ],
        compiler_params=pltpu.CompilerParams(
            collective_id=0, has_side_effects=True, vmem_limit_bytes=48 * 2**20),
        cost_estimate=pl.CostEstimate(flops=3 * 10**9, bytes_accessed=10**7, transcendentals=0),
        name="parafac2",
    )(visit_codes, slice_length, code_factor, mix_factor, slice_weight)
    return mix, code.reshape(512, 128), slices.reshape(n_code * 2, 128)


def solution(mesh):
    in_specs = (P("pat", None, "code"), P("pat"), P("code", None), P(), P("pat", None))
    out_specs = (P(), P("code", None), P("pat", None))
    body = functools.partial(shards, mesh.shape["pat"], mesh.shape["code"])
    return jax.shard_map(body, mesh=mesh, in_specs=in_specs, out_specs=out_specs, check_vma=False)
```

time: 336 us -> 84.6 us (0.25); the launches traced: 332 us -> 84.4 us
  waiting for transfers between devices: 223 us -> 0 us
  matrix products: 82.9 us -> 0 us
  Pallas kernels: 0 us -> 78.8 us
  between operations: 14.6 us -> 0.65 us
  other arithmetic: 7.06 us -> 0 us
    psum x2 -> x0, waiting for transfers between devices: 223 us -> none  [the longest x1 112 us: shards(): local_a = lax.psum(partial_a, 'code')]
    dot_general x34 -> x0, matrix products: 82.9 us -> none  [the longest x16 25.6 us: newton_schulz(): inner = jnp.einsum('kar,kab,kbs->krs', multi, grams, multi, precision=HIGH)]
    pallas_call x0 -> x1, Pallas kernels: none -> 78.8 us  [shards(): pl.pallas_call(functools.partial(kernel, n_pat, n_code), out_shape=(jax.S...]
    select_n x1 -> x0, other arithmetic: 4.67 us -> none  [shards(): jnp.where(live[:, :, None], visit_codes, jnp.zeros_like(visit_codes))]
  transfers between devices with their start and end apart: 2 -> 0, of which waited for: 2 -> 0; matrix products, arithmetic and copies ran while one was open for 0% -> 0% of each run, Pallas kernels for 0% -> 0%
where the time goes in v1:
time: 84.6 us; the launch traced here: 84.4 us
  Pallas kernels  78.8 us (93%)
  local copies, waits for them, and re-layouts  4.94 us (6%)
    pallas_call x1, Pallas kernels, shards(): pl.pallas_call(functools.partial(kernel, n_pat, n_code), out_shape=(jax.S...  78.8 us
    unnamed x11, local copies, waits for them, and re-layouts  4.94 us

profile of v1, /device:TPU:1, one launch (start us, length us, event | category | flops | bytes accessed | tf_op | source)
XLA Modules:
  0.0 84.4 jit_solution(8913328551492142899)
XLA Ops:
  0.6 0.0 copy-start
  0.6 0.9 %copy-done = bf16[512,128]{1,0:T(8,128)(2,1)S(1)} copy-done((bf16[512,128]{1,0:T(8,128)(2,1)S(1)}, bf16[512,128]{1,0:T(8,128)(2,1)}, u32[]{:S(2)}) %copy-start) | copy-done | bytes 131096
  1.5 0.0 copy-start.1
  1.5 0.8 copy-done.1
  2.3 0.0 copy-start.2
  2.3 0.7 copy-done.2
  3.0 0.0 copy-start.3
  3.0 0.7 copy-done.3
  3.6 78.8 %parafac2.1 = (f32[128,128]{1,0:T(8,128)S(1)}, f32[2,16,16,128]{3,2,1,0:T(8,128)S(1)}, f32[8,2,128]{2,1,0:T(2,128)S(1)}) custom-call(bf16[64,128,512]{2,1,0:T(8,128)(2,1)} %x_hbm.1, s32[16]{0:T(128)S(1)} %copy-done.3, bf16[512,128]{1,0:T(8,128)(2,1)S(1)} %copy-done, bf16[128,128]{1,0:T(8,128)(2,1)S(1)} %copy-done.1, f32[16,128]{1,0:T(8,128)S(1)} %copy-done.2), custom_call_target="tpu_custom_call" | custom-call | flops 3000000000 | bytes 10000000 | tf_op jit(solution)/shard_map/parafac2/pallas_call | solution.py:348
  82.4 0.6 copy.11
  83.1 0.7 copy.12
  83.8 0.6 copy.13
Async XLA Ops:
  0.6 0.9 %copy-start = (bf16[512,128]{1,0:T(8,128)(2,1)S(1)}, bf16[512,128]{1,0:T(8,128)(2,1)}, u32[]{:S(2)}) copy-start(bf16[512,128]{1,0:T(8,128)(2,1)} %v_ref.1) | copy-start | bytes 393220
  1.5 0.8 copy-start.1
  2.3 0.7 copy-start.2
  3.0 0.7 copy-start.3

commit v2 on v1

--- a/solution.py
+++ b/solution.py
@@ -36,13 +36,19 @@
     return codes.reshape(128, 128).astype(jnp.int16), power
 
 
-def kernel(n_pat, n_code, x_hbm, len_ref, v_ref, h_ref, d_ref,
+def kernel(n_pat, n_code, x_hbm, len_hbm, v_hbm, h_hbm, d_hbm,
            mix_ref, code_ref, slice_ref,
-           xv, ap, starts, rs_send, rs_recv, a_sum, u_own, u_recv, acc,
-           mixp, m1, mz, m2, m3, slp, slr, acct, cbuf, hsum, rbuf,
-           x_sem, rs_ss, rs_rs, ag_ss, ag_rs, m1_ss, m1_rs, m2_ss, m2_rs,
-           m3_ss, m3_rs, m4_ss, m4_rs, sl_ss, sl_rs, c_ss, c_rs, r_ss, r_rs,
+           len_ref, v_ref, h_ref, d_ref, in_sem, xv, ap, starts, rs_send, rs_recv, a_sum, u_own, u_recv, acc,
+           mixp, m2, m3s, m3r, zx, slp, acct, cbuf, hsum, rbuf,
+           x_sem, rs_ss, rs_rs, ag_ss, ag_rs, zx_ss, zx_rs, m2_ss, m2_rs,
+           m3_ss, m3_rs, m4_ss, m4_rs, c_ss, c_rs, r_ss, r_rs,
            g_ss, g_rs, f_ss, f_rs):
+    sent = []
+
+    def send(copy):
+        copy.start()
+        sent.append(copy)
+
     pat = lax.axis_index("pat")
     me = lax.axis_index("code")
     chips = n_pat // 2
@@ -66,8 +72,19 @@
         part = pl.ds(i * 4, 4)
         return pltpu.make_async_copy(x_hbm.at[part], xv.at[part], x_sem.at[i])
 
-    for i in range(16):
+    small = [
+        pltpu.make_async_copy(src, dst, in_sem.at[i])
+        for i, (src, dst) in enumerate(
+            [(len_hbm, len_ref), (v_hbm, v_ref), (h_hbm, h_ref), (d_hbm, d_ref)])
+    ]
+    small[1].start()
+    x_copy(0).start()
+    for i in (0, 2, 3):
+        small[i].start()
+    for i in range(1, 16):
         x_copy(i).start()
+    for copy in small:
+        copy.wait()
     at = jnp.int32(0)
     for k in range(16):
         starts[k] = at
@@ -76,15 +93,14 @@
     @pl.loop(0, 16)
     def _(i):
         x_copy(i).wait()
-        part = pl.ds(i * 4, 4)
-        ap[part] = dot(xv[part].reshape(512, 512), v_ref[...]).reshape(4, 128, 128)
 
     pl.semaphore_wait(barrier, n_code - 1 + chips)
 
     rowpos = lax.broadcasted_iota(jnp.int32, (128, 128), 0)
 
-    def own(s, j):
-        block = ap[jnp.minimum(starts[s] + j, 63)]
+    def own(s, j, early=False):
+        at = jnp.minimum(starts[s] + j, 63)
+        block = dot(xv[at], v_ref[...]) if early else ap[at]
         return jnp.where(rowpos < len_ref[s] - j * 128, block, 0.0)
 
     def received(buf, j):
@@ -108,20 +124,29 @@
         at = (way * 4 + step) * 2 + half
         powers = []
         for j in range(4):
-            rows = own(dest * 2 + half, j)
+            rows = own(dest * 2 + half, j, step <= first)
             if step > first:
                 rows = rows + received(rs_recv.at[at - 2], j)
             codes, power = encode(rows)
             rs_send[at, 128 * j:128 * j + 128] = codes
             powers.append(power)
         rs_send[at, 512:528] = jnp.concatenate(powers, axis=0).astype(jnp.int32).astype(jnp.int16)
-        rs_copy(way, step, half).start()
+        send(rs_copy(way, step, half))
 
     rs_message(0, 0, 0)
     rs_message(1, 0, 1)
+    rs_message(0, 1, 1)
+    rs_message(1, 1, 0)
+
+    @pl.loop(0, 16)
+    def _(i):
+        part = pl.ds(i * 4, 4)
+        ap[part] = dot(xv[part].reshape(512, 512), v_ref[...]).reshape(4, 128, 128)
+
     for step in range(1, 4):
-        rs_message(0, step, 1)
-        rs_message(1, step, 0)
+        if step > 1:
+            rs_message(0, step, 1)
+            rs_message(1, step, 0)
         rs_message(0, step, 0)
         rs_message(1, step, 1)
 
@@ -190,10 +215,10 @@
             send_sem=ag_ss.at[at], recv_sem=ag_rs.at[at],
             device_id=(pat, to), device_id_type=MESH)
 
-    ag_copy(0, 0, 0).start()
-    ag_copy(1, 0, 1).start()
-    ag_copy(0, 0, 1).start()
-    ag_copy(1, 0, 0).start()
+    send(ag_copy(0, 0, 0))
+    send(ag_copy(1, 0, 1))
+    send(ag_copy(0, 0, 1))
+    send(ag_copy(1, 0, 0))
 
     def code_term(u, s):
         first = starts[s]
@@ -206,40 +231,34 @@
         [jnp.sum(h32 * ws[half], axis=0, keepdims=True) for half in range(2)]
         + [jnp.zeros((6, 128), F32)], axis=0)
 
-    def sl_copy(off):
-        return pltpu.make_async_remote_copy(
-            src_ref=slp, dst_ref=slr.at[off - 1], send_sem=sl_ss.at[off - 1], recv_sem=sl_rs.at[off - 1],
+    def m2_copy():
+        return pltpu.make_async_remote_copy(
+            src_ref=mixp, dst_ref=m2, send_sem=m2_ss, recv_sem=m2_rs,
+            device_id=(other, me), device_id_type=MESH)
+
+    def m3_copy(off):
+        to = chip_at(off)
+        return pltpu.make_async_remote_copy(
+            src_ref=m3s.at[to], dst_ref=m3r.at[chip],
+            send_sem=m3_ss.at[off - 1], recv_sem=m3_rs.at[off - 1],
+            device_id=(to * 2 + core, me), device_id_type=MESH)
+
+    def zx_copy(off):
+        return pltpu.make_async_remote_copy(
+            src_ref=zx.at[me], dst_ref=zx.at[me],
+            send_sem=zx_ss.at[off - 1], recv_sem=zx_rs.at[off - 1],
             device_id=(pat, z_at(off)), device_id_type=MESH)
 
-    def m1_copy(off):
-        to = z_at(off)
-        return pltpu.make_async_remote_copy(
-            src_ref=mixp.at[pl.ds(pl.multiple_of(to * 16, 16), 16)], dst_ref=m1.at[off - 1],
-            send_sem=m1_ss.at[off - 1], recv_sem=m1_rs.at[off - 1],
-            device_id=(pat, to), device_id_type=MESH)
-
-    def m2_copy():
-        return pltpu.make_async_remote_copy(
-            src_ref=mz, dst_ref=m2, send_sem=m2_ss, recv_sem=m2_rs,
-            device_id=(other, me), device_id_type=MESH)
-
-    def m3_copy(off, sender):
-        return pltpu.make_async_remote_copy(
-            src_ref=m3.at[sender], dst_ref=m3.at[sender],
-            send_sem=m3_ss.at[off - 1], recv_sem=m3_rs.at[off - 1],
+    mix_rows = 128 // chips
+
+    def m4_copy(off):
+        at = pl.ds(pl.multiple_of(chip * mix_rows, mix_rows), mix_rows)
+        return pltpu.make_async_remote_copy(
+            src_ref=mix_ref.at[at], dst_ref=mix_ref.at[at],
+            send_sem=m4_ss.at[off - 1], recv_sem=m4_rs.at[off - 1],
             device_id=(chip_at(off) * 2 + core, me), device_id_type=MESH)
 
-    def m4_copy(off, rows):
-        part = pl.ds(pl.multiple_of(rows * 16, 16), 16)
-        return pltpu.make_async_remote_copy(
-            src_ref=mix_ref.at[part], dst_ref=mix_ref.at[part],
-            send_sem=m4_ss.at[off - 1], recv_sem=m4_rs.at[off - 1],
-            device_id=(pat, z_at(off)), device_id_type=MESH)
-
-    for off in range(1, n_code):
-        m1_copy(off).start()
-        sl_copy(off).start()
-
+    send(m2_copy())
     acc[...] = code_term(u_own[0], me * 2) + code_term(u_own[1], me * 2 + 1)
 
     for step in range(4):
@@ -248,40 +267,31 @@
                 continue
             ag_copy(way, step, half).wait_recv()
             if step < 2 or (step == 2 and half == way):
-                ag_copy(way, step + 1, half).start()
+                send(ag_copy(way, step + 1, half))
             owner = z_at(-step - 1) if way == 0 else z_at(step + 1)
             acc[...] += code_term(u_recv[(way * 4 + step) * 2 + half], owner * 2 + half)
-        if step == 0:
-            total = mixp[pl.ds(pl.multiple_of(me * 16, 16), 16), :]
-            for off in range(1, n_code):
-                m1_copy(off).wait_recv()
-                total = total + m1[off - 1]
-            mz[...] = total
-            m2_copy().start()
-            slice_ref[me] = slp[0:2]
-            for off in range(1, n_code):
-                sl_copy(off).wait_recv()
-                slice_ref[z_at(-off)] = slr[off - 1, 0:2]
-        if step == 1:
-            m2_copy().wait_recv()
-            m3[chip] = mz[...] + m2[...]
-            for off in range(1, chips):
-                m3_copy(off, chip).start()
-        if step == 2:
-            for off in range(1, chips):
-                m3_copy(off, chip_at(-off)).wait_recv()
-            total = m3[0]
-            for c in range(1, chips):
-                total = total + m3[c]
-            mix_ref[pl.ds(pl.multiple_of(me * 16, 16), 16), :] = total
-            for off in range(1, n_code):
-                m4_copy(off, me).start()
+            if (step, way, half) == (0, 1, 1):
+                m2_copy().wait_recv()
+                m3s[...] = (mixp[...] + m2[...]).reshape(chips, mix_rows, 128)
+                m3r[chip] = m3s[chip]
+                for off in range(1, chips):
+                    send(m3_copy(off))
+            if (step, way, half) == (2, 1, 1):
+                for off in range(1, chips):
+                    m3_copy(off).wait_recv()
+                total = m3r[0]
+                for c in range(1, chips):
+                    total = total + m3r[c]
+                zx[me, 0:mix_rows] = total
+                zx[me, mix_rows:mix_rows + 8] = slp[...]
 
     acct[...] = acc[...].T.reshape(2, 256, 128)
     core_copy = pltpu.make_async_remote_copy(
         src_ref=acct.at[1 - core], dst_ref=cbuf, send_sem=c_ss, recv_sem=c_rs,
         device_id=(other, me), device_id_type=MESH)
-    core_copy.start()
+    send(core_copy)
+    for off in range(1, n_code):
+        send(zx_copy(off))
     core_copy.wait_recv()
     hsum[...] = (acct[core] + cbuf[...]).reshape(chips, 256 // chips, 128)
 
@@ -293,7 +303,17 @@
             device_id=(to * 2 + core, me), device_id_type=MESH)
 
     for off in range(1, chips):
-        r_copy(off).start()
+        send(r_copy(off))
+    for off in range(1, n_code):
+        zx_copy(off).wait_recv()
+    total = zx[0, 0:mix_rows]
+    for z in range(1, n_code):
+        total = total + zx[z, 0:mix_rows]
+    mix_ref[pl.ds(pl.multiple_of(chip * mix_rows, mix_rows), mix_rows), :] = total
+    for off in range(1, chips):
+        send(m4_copy(off))
+    for z in range(n_code):
+        slice_ref[z] = zx[z, mix_rows:mix_rows + 2]
     total = hsum[chip]
     for off in range(1, chips):
         r_copy(off).wait_recv()
@@ -307,7 +327,7 @@
             device_id=(chip_at(off) * 2 + core, me), device_id_type=MESH)
 
     for off in range(1, chips):
-        g_copy(off, chip).start()
+        send(g_copy(off, chip))
     for off in range(1, chips):
         g_copy(off, chip_at(-off)).wait_recv()
 
@@ -316,28 +336,12 @@
             src_ref=code_ref.at[half], dst_ref=code_ref.at[half], send_sem=f_ss, recv_sem=f_rs,
             device_id=(other, me), device_id_type=MESH)
 
-    f_copy(core).start()
-    for off in range(1, n_code):
-        m4_copy(off, z_at(-off)).wait_recv()
-
-    for way in range(2):
-        for step in range(4):
-            for half in range(2):
-                if half == way or step > 0:
-                    rs_copy(way, step, half).wait_send()
-                if half == way or step < 3:
-                    ag_copy(way, step, half).wait_send()
-    for off in range(1, n_code):
-        m1_copy(off).wait_send()
-        sl_copy(off).wait_send()
-        m4_copy(off, me).wait_send()
-    m2_copy().wait_send()
-    core_copy.wait_send()
-    for off in range(1, chips):
-        m3_copy(off, chip).wait_send()
-        r_copy(off).wait_send()
-        g_copy(off, chip).wait_send()
-    f_copy(core).wait_send()
+    send(f_copy(core))
+    for off in range(1, chips):
+        m4_copy(off).wait_recv()
+
+    for copy in sent:
+        copy.wait_send()
     f_copy(1 - core).wait_recv()
 
 
@@ -352,9 +356,14 @@
             jax.ShapeDtypeStruct((2, chips, 256 // chips, 128), F32),
             jax.ShapeDtypeStruct((n_code, 2, 128), F32),
         ),
-        in_specs=[pl.BlockSpec(memory_space=pl.ANY), pl.BlockSpec(memory_space=pltpu.SMEM), vmem, vmem, vmem],
+        in_specs=[pl.BlockSpec(memory_space=pltpu.HBM)] * 5,
         out_specs=(vmem, vmem, vmem),
         scratch_shapes=[
+            pltpu.SMEM((16,), jnp.int32),
+            pltpu.VMEM((512, 128), BF16),
+            pltpu.VMEM((128, 128), BF16),
+            pltpu.VMEM((16, 128), F32),
+            dma((4,)),
             pltpu.VMEM((64, 128, 512), BF16),
             pltpu.VMEM((64, 128, 128), F32),
             pltpu.SMEM((16,), jnp.int32),
@@ -365,12 +374,11 @@
             pltpu.VMEM((16, 128, 512), BF16),
             pltpu.VMEM((128, 512), F32),
             pltpu.VMEM((128, 128), F32),
-            pltpu.VMEM((n_code - 1, 16, 128), F32),
-            pltpu.VMEM((16, 128), F32),
-            pltpu.VMEM((16, 128), F32),
-            pltpu.VMEM((chips, 16, 128), F32),
+            pltpu.VMEM((128, 128), F32),
+            pltpu.VMEM((chips, 128 // chips, 128), F32),
+            pltpu.VMEM((chips, 128 // chips, 128), F32),
+            pltpu.VMEM((n_code, 128 // chips + 8, 128), F32),
             pltpu.VMEM((8, 128), F32),
-            pltpu.VMEM((n_code - 1, 8, 128), F32),
             pltpu.VMEM((2, 256, 128), F32),
             pltpu.VMEM((256, 128), F32),
             pltpu.VMEM((chips, 256 // chips, 128), F32),
@@ -381,8 +389,7 @@
             dma((n_code - 1,)), dma((n_code - 1,)),
             dma, dma,
             dma((chips - 1,)), dma((chips - 1,)),
-            dma((n_code - 1,)), dma((n_code - 1,)),
-            dma((n_code - 1,)), dma((n_code - 1,)),
+            dma((chips - 1,)), dma((chips - 1,)),
             dma, dma,
             dma((chips - 1,)), dma((chips - 1,)),
             dma((chips - 1,)), dma((chips - 1,)),

time: 84.6 us -> 80.9 us (0.956)
  Pallas kernels: 78.8 us -> 75.1 us
    pallas_call x1, Pallas kernels: 78.8 us -> 75.1 us  [shards(): pl.pallas_call(functools.partial(kernel, n_pat, n_code), out_shape=(jax.S...]
where the time goes in v2:
time: 80.9 us; the launch traced here: 80.7 us
  Pallas kernels  75.1 us (93%)
  local copies, waits for them, and re-layouts  4.94 us (6%)
    pallas_call x1, Pallas kernels, shards(): pl.pallas_call(functools.partial(kernel, n_pat, n_code), out_shape=(jax.S...  75.1 us
    unnamed x11, local copies, waits for them, and re-layouts  4.94 us

profile of v2, /device:TPU:1, one launch (start us, length us, event | category | flops | bytes accessed | tf_op | source)
XLA Modules:
  0.0 80.7 jit_solution(7112592839606621995)
XLA Ops:
  0.6 0.0 copy-start
  0.6 0.9 %copy-done = bf16[512,128]{1,0:T(8,128)(2,1)S(1)} copy-done((bf16[512,128]{1,0:T(8,128)(2,1)S(1)}, bf16[512,128]{1,0:T(8,128)(2,1)}, u32[]{:S(2)}) %copy-start) | copy-done | bytes 131096
  1.5 0.0 copy-start.1
  1.5 0.8 copy-done.1
  2.3 0.0 copy-start.2
  2.3 0.7 copy-done.2
  3.0 0.0 copy-start.3
  3.0 0.7 copy-done.3
  3.6 75.1 %parafac2.1 = (f32[128,128]{1,0:T(8,128)S(1)}, f32[2,16,16,128]{3,2,1,0:T(8,128)S(1)}, f32[8,2,128]{2,1,0:T(2,128)S(1)}) custom-call(bf16[64,128,512]{2,1,0:T(8,128)(2,1)} %x_hbm.1, s32[16]{0:T(128)S(1)} %copy-done.3, bf16[512,128]{1,0:T(8,128)(2,1)S(1)} %copy-done, bf16[128,128]{1,0:T(8,128)(2,1)S(1)} %copy-done.1, f32[16,128]{1,0:T(8,128)S(1)} %copy-done.2), custom_call_target="tpu_custom_call" | custom-call | flops 3000000000 | bytes 10000000 | tf_op jit(solution)/shard_map/parafac2/pallas_call | solution.py:352
  78.7 0.6 copy.11
  79.4 0.7 copy.12
  80.1 0.6 copy.13
Async XLA Ops:
  0.6 0.9 %copy-start = (bf16[512,128]{1,0:T(8,128)(2,1)S(1)}, bf16[512,128]{1,0:T(8,128)(2,1)}, u32[]{:S(2)}) copy-start(bf16[512,128]{1,0:T(8,128)(2,1)} %v_hbm.1) | copy-start | bytes 393220
  1.5 0.8 copy-start.1
  2.3 0.7 copy-start.2
  3.0 0.7 copy-start.3

commit v3 on v2

--- a/solution.py
+++ b/solution.py
@@ -60,13 +60,6 @@
 
     def chip_at(off):
         return lax.rem(chip + off + chips, chips)
-
-    barrier = pltpu.get_barrier_semaphore()
-    for off in range(1, n_code):
-        pl.semaphore_signal(barrier, inc=1, device_id=(pat, z_at(off)), device_id_type=MESH)
-    pl.semaphore_signal(barrier, inc=1, device_id=(other, me), device_id_type=MESH)
-    for off in range(1, chips):
-        pl.semaphore_signal(barrier, inc=1, device_id=(chip_at(off) * 2 + core, me), device_id_type=MESH)
 
     def x_copy(i):
         part = pl.ds(i * 4, 4)
@@ -83,6 +76,13 @@
         small[i].start()
     for i in range(1, 16):
         x_copy(i).start()
+    barrier = pltpu.get_barrier_semaphore()
+    for off in range(1, n_code):
+        pl.semaphore_signal(barrier, inc=1, device_id=(pat, z_at(off)), device_id_type=MESH)
+    pl.semaphore_signal(barrier, inc=1, device_id=(other, me), device_id_type=MESH)
+    for off in range(1, chips):
+        pl.semaphore_signal(barrier, inc=1, device_id=(chip_at(off) * 2 + core, me), device_id_type=MESH)
+
     for copy in small:
         copy.wait()
     at = jnp.int32(0)
@@ -161,14 +161,15 @@
         dcol.append(jnp.sum(eye * drow[half], axis=1, keepdims=True))
 
     grams = []
-    for half in (1, 0):
-        rs_copy(0, 3, half).wait_recv()
-        rs_copy(1, 3, half).wait_recv()
+    for half in range(2):
+        rs_copy(1 - half, 3, half).wait_recv()
         for j in range(4):
-            rows = own(me * 2 + half, j)
-            rows = rows + received(rs_recv.at[6 + half], j)
-            rows = rows + received(rs_recv.at[14 + half], j)
+            rows = own(me * 2 + half, j) + received(rs_recv.at[(1 - half) * 8 + 6 + half], j)
             a_sum[half, 128 * j:128 * j + 128] = rows
+    for half in range(2):
+        rs_copy(half, 3, half).wait_recv()
+        for j in range(4):
+            a_sum[half, 128 * j:128 * j + 128] += received(rs_recv.at[half * 8 + 6 + half], j)
     ahs, als, aths, atls = [], [], [], []
     for half in range(2):
         ah, al = split(a_sum[half])

time: 80.9 us -> 80.8 us (level)
  no operation moved by 1% of the time
where the time goes in v3:
time: 80.8 us; the launch traced here: 80.6 us
  Pallas kernels  75 us (93%)
  local copies, waits for them, and re-layouts  4.94 us (6%)
    pallas_call x1, Pallas kernels, shards(): pl.pallas_call(functools.partial(kernel, n_pat, n_code), out_shape=(jax.S...  75 us
    unnamed x11, local copies, waits for them, and re-layouts  4.94 us

profile of v3, /device:TPU:1, one launch (start us, length us, event | category | flops | bytes accessed | tf_op | source)
XLA Modules:
  0.0 80.6 jit_solution(2174778808973408446)
XLA Ops:
  0.6 0.0 copy-start
  0.6 0.9 %copy-done = bf16[512,128]{1,0:T(8,128)(2,1)S(1)} copy-done((bf16[512,128]{1,0:T(8,128)(2,1)S(1)}, bf16[512,128]{1,0:T(8,128)(2,1)}, u32[]{:S(2)}) %copy-start) | copy-done | bytes 131096
  1.5 0.0 copy-start.1
  1.5 0.8 copy-done.1
  2.3 0.0 copy-start.2
  2.3 0.7 copy-done.2
  3.0 0.0 copy-start.3
  3.0 0.7 copy-done.3
  3.6 75.0 %parafac2.1 = (f32[128,128]{1,0:T(8,128)S(1)}, f32[2,16,16,128]{3,2,1,0:T(8,128)S(1)}, f32[8,2,128]{2,1,0:T(2,128)S(1)}) custom-call(bf16[64,128,512]{2,1,0:T(8,128)(2,1)} %x_hbm.1, s32[16]{0:T(128)S(1)} %copy-done.3, bf16[512,128]{1,0:T(8,128)(2,1)S(1)} %copy-done, bf16[128,128]{1,0:T(8,128)(2,1)S(1)} %copy-done.1, f32[16,128]{1,0:T(8,128)S(1)} %copy-done.2), custom_call_target="tpu_custom_call" | custom-call | flops 3000000000 | bytes 10000000 | tf_op jit(solution)/shard_map/parafac2/pallas_call | solution.py:353
  78.7 0.6 copy.11
  79.3 0.7 copy.12
  80.0 0.6 copy.13
Async XLA Ops:
  0.6 0.9 %copy-start = (bf16[512,128]{1,0:T(8,128)(2,1)S(1)}, bf16[512,128]{1,0:T(8,128)(2,1)}, u32[]{:S(2)}) copy-start(bf16[512,128]{1,0:T(8,128)(2,1)} %v_hbm.1) | copy-start | bytes 393220
  1.5 0.8 copy-start.1
  2.3 0.7 copy-start.2
  3.0 0.7 copy-start.3
